TPU v7x, 32 devices: a whole 2x2x4 slice. The times are simulated.
32 devices in a mesh: groups: 2 (over x), wide: 8 (over z, y), narrow: 2 (over core).
Axes of the slice: x: 2, y: 2, z: 4, core: 2. Of those that a mesh axis runs over, the one named last changes fastest.
Arguments:
- volume: bfloat16 [32, 128, 16, 32], P(None, ('groups', 'wide'), None, 'narrow'), parts along dimension 1, may hold values from -6 to 6
- cotangent: bfloat16 [32, 128, 16, 32], P(None, ('groups', 'wide'), None, 'narrow'), parts along dimension 1, may hold values from -6 to 6
- fine_weight: bfloat16 [27, 32, 32], replicated, may hold values from -0.21875 to 0.21875
- merge_weight: bfloat16 [16384, 1024], P('wide'), may hold values from -0.046875 to 0.046875
- hidden_weight: bfloat16 [27, 1024, 2048], P(None, None, 'wide'), may hold values from -0.0390625 to 0.0390625
- step_table: float32 [1000, 2048], P(None, 'wide'), may hold values from -6 to 6
- output_weight: bfloat16 [27, 2048, 1024], P(None, 'wide'), may hold values from -0.02734375 to 0.02734375
- expand_weight: bfloat16 [1024, 16384], P(None, 'wide'), may hold values from -0.1875 to 0.1875
- timestep: int32 [2], P('groups'), parts along dimension 0, may hold values from 0 to 999
Outputs:
- input_grad: bfloat16 [32, 128, 16, 32], P(None, ('groups', 'wide'), None, 'narrow'), parts along dimension 1
There are 2 independent parts, one for each index of `groups`. A program takes and returns all parts, laid end to end along the dimension named above; an argument that names none is the same for every part. Nothing has to cross between parts.
All inputs are finite; a program needn't handle non-finite values.
Results may differ from a plain program's by a relative error of at most 0.012.
Values may be sent and summed in bfloat16 or wider, within the bound.
No kernel may reach another device: no remote copies, remote signals or barrier semaphores. Data moves between devices by JAX's collectives and lax.ppermute only.
A program may use at most 128 MiB of HBM per device.

v0:
```python
import jax
import jax.numpy as jnp
from jax import lax
from jax.sharding import PartitionSpec as P

PATCH = 8


def extended(cells, sides, width):
    for axis, dim in sides:
        count = lax.axis_size(axis)
        ends = count - 1
        head = lax.slice_in_dim(cells, 0, width, axis=dim)
        tail = lax.slice_in_dim(cells, cells.shape[dim] - width, cells.shape[dim], axis=dim)
        cells = jnp.concatenate(
            [
                lax.ppermute(tail, axis, [(i, (i + 1) % count) for i in range(ends)]),
                cells,
                lax.ppermute(head, axis, [((i + 1) % count, i) for i in range(ends)]),
            ],
            axis=dim,
        )
    return cells


def shifts(transposed):
    return [
        (2 - i, 2 - j, 2 - k) if transposed else (i, j, k)
        for i in range(3)
        for j in range(3)
        for k in range(3)
    ]


def silu_slope(values):
    logistic = jax.nn.sigmoid(values)
    return logistic * (1.0 + values * (1.0 - logistic))


def fine_conv(fine_field, weight, transposed):
    grown = extended(fine_field, (("wide", 1), ("narrow", 3)), 1)
    padded = jnp.pad(grown, ((0, 0), (0, 0), (1, 1), (0, 0)))
    kernel = weight.reshape(3, 3, 3, weight.shape[1], weight.shape[2])
    if transposed:
        kernel = kernel[::-1, ::-1, ::-1]
    result = lax.conv_general_dilated(
        padded[None],
        kernel,
        (1, 1, 1),
        "VALID",
        dimension_numbers=("NCDHW", "DHWIO", "NCDHW"),
        preferred_element_type=jnp.float32,
    )
    return result[0]


def to_patches(fine_field):
    channels = fine_field.shape[0]
    shaped = fine_field.reshape(
        channels, PATCH, fine_field.shape[2] // PATCH, PATCH, fine_field.shape[3] // PATCH, PATCH
    )
    return shaped.transpose(2, 4, 1, 3, 5, 0).reshape(-1, PATCH**3 * channels)


def send_patches(fine_field):
    return lax.all_to_all(to_patches(fine_field), "wide", split_axis=1, concat_axis=0, tiled=True)


def return_patches(patch_rows, fine_height, fine_depth, channels):
    returned = lax.all_to_all(patch_rows, "wide", split_axis=0, concat_axis=1, tiled=True)
    shaped = returned.reshape(
        fine_height // PATCH, fine_depth // PATCH, PATCH, PATCH, PATCH, channels
    )
    return shaped.transpose(5, 2, 0, 3, 1, 4).reshape(channels, PATCH, fine_height, fine_depth)


def coarse_faces(coarse_block):
    return extended(coarse_block, (("narrow", 2),), 1)


def wide_input_conv(coarse_block, weight_mat, out_count, transposed):
    grown = coarse_faces(coarse_block)
    products = jnp.einsum("xyzd,dk->xyzk", grown, weight_mat, preferred_element_type=jnp.float32)
    padded = jnp.pad(products, ((1, 1), (1, 1), (0, 0), (0, 0)))
    extent = coarse_block.shape[:3]
    summed = jnp.zeros(extent + (out_count,), jnp.float32)
    for tap_index, (a, b, c) in enumerate(shifts(transposed)):
        summed = (
            summed
            + padded[
                a : a + extent[0],
                b : b + extent[1],
                c : c + extent[2],
                tap_index * out_count : (tap_index + 1) * out_count,
            ]
        )
    return summed


def narrow_input_conv(coarse_block, weight_mat, transposed):
    grown = coarse_faces(coarse_block)
    padded = jnp.pad(grown, ((1, 1), (1, 1), (0, 0), (0, 0)))
    extent = coarse_block.shape[:3]
    columns = jnp.concatenate(
        [
            padded[a : a + extent[0], b : b + extent[1], c : c + extent[2]]
            for a, b, c in shifts(transposed)
        ],
        axis=3,
    )
    return jnp.einsum("xyzk,kd->xyzd", columns, weight_mat, preferred_element_type=jnp.float32)


def shards(
    volume,
    cotangent,
    fine_weight,
    merge_weight,
    hidden_weight,
    step_table,
    output_weight,
    expand_weight,
    timestep,
):
    channels = volume.shape[0]
    fine_height = volume.shape[2]
    fine_depth = volume.shape[3]
    wide_count = lax.axis_size("wide")
    features = merge_weight.shape[1]
    hidden_local = hidden_weight.shape[2]
    coarse_grid = (wide_count, fine_height // PATCH, fine_depth // PATCH)
    hidden_mat = hidden_weight.transpose(1, 0, 2).reshape(features, 27 * hidden_local)
    output_mat = output_weight.reshape(27 * hidden_local, features)
    output_back = output_weight.transpose(2, 0, 1).reshape(features, 27 * hidden_local)
    hidden_back = hidden_weight.transpose(0, 2, 1).reshape(27 * hidden_local, features)

    def total_rows(partial_value):
        return lax.psum(partial_value, "wide")

    pre_act = fine_conv(volume, fine_weight, False)
    activated = jax.nn.silu(pre_act).astype(jnp.bfloat16)
    received = send_patches(activated)
    merged = total_rows(jnp.dot(received, merge_weight, preferred_element_type=jnp.float32))
    coarse_in = merged.astype(jnp.bfloat16).reshape(coarse_grid + (features,))
    bias_row = step_table[timestep[0]]
    gate_pre = wide_input_conv(coarse_in, hidden_mat, hidden_local, False) + bias_row
    hidden_act = jax.nn.silu(gate_pre).astype(jnp.bfloat16)
    branch = total_rows(narrow_input_conv(hidden_act, output_mat, False).reshape(-1, features))
    residual_sum = (merged + branch).astype(jnp.bfloat16)
    expanded = jnp.dot(residual_sum, expand_weight, preferred_element_type=jnp.float32).astype(
        jnp.bfloat16
    )
    expanded_field = return_patches(expanded, fine_height, fine_depth, channels)
    combined = activated.astype(jnp.float32) + expanded_field.astype(jnp.float32)
    grad_comb = (cotangent.astype(jnp.float32) * silu_slope(combined)).astype(jnp.bfloat16)
    grad_res = total_rows(
        jnp.einsum(
            "nk,dk->nd", send_patches(grad_comb), expand_weight, preferred_element_type=jnp.float32
        )
    )
    grad_res_b = grad_res.astype(jnp.bfloat16).reshape(coarse_grid + (features,))
    grad_hidden = wide_input_conv(grad_res_b, output_back, hidden_local, True)
    grad_gate = (grad_hidden * silu_slope(gate_pre)).astype(jnp.bfloat16)
    grad_conv = total_rows(narrow_input_conv(grad_gate, hidden_back, True).reshape(-1, features))
    grad_merged = (grad_res + grad_conv).astype(jnp.bfloat16)
    grad_cells = jnp.einsum(
        "nd,kd->nk", grad_merged, merge_weight, preferred_element_type=jnp.float32
    ).astype(jnp.bfloat16)
    grad_act = return_patches(grad_cells, fine_height, fine_depth, channels).astype(
        jnp.float32
    ) + grad_comb.astype(jnp.float32)
    grad_pre = (grad_act * silu_slope(pre_act)).astype(jnp.bfloat16)
    return fine_conv(grad_pre, fine_weight.transpose(0, 2, 1), True).astype(jnp.bfloat16)


def solution(mesh):
    in_specs = (
        P(None, ("groups", "wide"), None, "narrow"),
        P(None, ("groups", "wide"), None, "narrow"),
        P(),
        P("wide", None),
        P(None, None, "wide"),
        P(None, "wide"),
        P(None, "wide", None),
        P(None, "wide"),
        P("groups"),
    )
    out_specs = P(None, ("groups", "wide"), None, "narrow")
    return jax.shard_map(shards, mesh=mesh, in_specs=in_specs, out_specs=out_specs, check_vma=False)
```

profile of v0, /device:TPU:0, one launch (start us, length us, event | category | flops | bytes accessed | tf_op | source)
XLA Modules:
  0.0 473.5 jit_solution(18221159646353453401)
XLA Ops:
  7.5 4.9 %collective-permute-start = (bf16[32,1,16,16]{0,3,2,1:T(8,128)(2,1)S(1)}, bf16[32,1,16,16]{0,3,2,1:T(8,128)(2,1)S(1)}, u32[]{:S(2)}, u32[]{:S(2)}) collective-permute-start(bf16[32,1,16,16]{0,3,2,1:T(8,128)(2,1)S(1)} %get-tuple-element.14), channel_id=1, source_target_pairs={{0,2},{2,4},{4,6},{6,8},{8,10},{10,12},{12,14},{1,3},{3,5},{5,7},{... | collective-permute-start | bytes 49160 | tf_op jit(solution)/shard_map/ppermute | solution.py:17
  15.4 3.2 collective-permute-done.1
  25.0 2.8 reshape.76
  28.8 2.4 fusion.20
  32.6 12.9 %all_to_all.64 = bf16[4,8,2048]{2,0,1:T(4,128)(2,1)S(1)} all-to-all(bf16[4,8,2048]{2,0,1:T(4,128)(2,1)S(1)} %copy.53), channel_id=1, replica_groups=mesh['groups'=2,'wide'=8,'narrow'=2] {'wide'}, dimensions={1} | all-to-all | bytes 262144 | tf_op jit(solution)/shard_map/all_to_all | solution.py:66
  45.5 3.7 fusion.129
  50.0 67.2 %all-reduce.11.cloned.1.call-done = f32[32,1024]{1,0:T(8,128)} async-done(((f32[32,1024]{1,0:T(8,128)}), f32[32,1024]{1,0:T(8,128)}) %all-reduce.11.cloned.1.call-update) | async-done | bytes 131088 | tf_op jit(solution)/shard_map/psum | solution.py:138
  120.7 18.6 %copy.57 = bf16[27,1024,256]{1,2,0:T(8,128)(2,1)} copy(bf16[27,1024,256]{2,1,0:T(8,128)(2,1)} %param.13) | data formatting | bytes 28311552 | tf_op args[4]
  139.4 9.4 %fusion.50 = f32[8,2,4,6912]{3,0,2,1:T(8,128)S(1)} fusion(bf16[1024,6912,1,1]{0,1,3,2:T(8,128)(2,1)} %bitcast.118, bf16[8,2,1,1024]{3,0,2,1:T(8,128)(2,1)S(1)} %collective-permute-done.5, bf16[8,2,2,1024]{3,0,2,1:T(8,128)(2,1)S(1)} %copy.54, bf16[8,2,1,1024]{3,0,2,1:T(8,128)(2,1)S(1)} %collective-permute-done.4), kind=kOutput, calls=%fused_computation.119 | convolution fusion | flops 906100736 | bytes 16056320 | tf_op jit(solution)/shard_map/xyzd,dk->xyzk/dot_general | solution.py:83
  148.9 3.0 collective-permute-start.6
  155.9 8.3 %fusion.130 = f32[32,1024]{1,0:T(8,128)} fusion(bf16[32,6912]{1,0:T(8,128)(2,1)S(1)} %dot_general.30, bf16[6912,1024]{1,0:T(8,128)(2,1)} %bitcast.120), kind=kOutput, calls=%fused_computation.271 | convolution fusion | flops 452984832 | bytes 14729216 | tf_op jit(solution)/shard_map/xyzk,kd->xyzd/dot_general | solution.py:111
  164.3 69.0 %all-reduce.13.cloned.1.call-done = f32[32,1024]{1,0:T(8,128)} async-done(((f32[32,1024]{1,0:T(8,128)}), f32[32,1024]{1,0:T(8,128)}) %all-reduce.13.cloned.1.call-update) | async-done | bytes 131088 | tf_op jit(solution)/shard_map/psum | solution.py:138
  233.3 3.1 convolution_convert_fusion.1
  236.4 11.1 %all_to_all.65 = bf16[8,4,2048]{2,1,0:T(4,128)(2,1)S(1)} all-to-all(bf16[8,4,2048]{2,1,0:T(4,128)(2,1)S(1)} %all_to_all.52), channel_id=1, replica_groups=mesh['groups'=2,'wide'=8,'narrow'=2] {'wide'}, dimensions={0} | all-to-all | bytes 262144 | tf_op jit(solution)/shard_map/all_to_all | solution.py:70
  251.9 9.7 %all_to_all.66 = bf16[4,8,2048]{2,0,1:T(4,128)(2,1)S(1)} all-to-all(bf16[4,8,2048]{2,0,1:T(4,128)(2,1)S(1)} %copy.62), channel_id=1, replica_groups=mesh['groups'=2,'wide'=8,'narrow'=2] {'wide'}, dimensions={1} | all-to-all | bytes 262144 | tf_op jit(solution)/shard_map/all_to_all | solution.py:66
  261.6 4.2 fusion.131
  265.9 67.4 %all-reduce.15.cloned.1.call-done = f32[32,1024]{1,0:T(8,128)} async-done(((f32[32,1024]{1,0:T(8,128)}), f32[32,1024]{1,0:T(8,128)}) %all-reduce.15.cloned.1.call-update) | async-done | bytes 131088 | tf_op jit(solution)/shard_map/psum | solution.py:138
  338.7 9.4 %fusion.56 = f32[8,2,4,6912]{3,0,2,1:T(8,128)S(1)} fusion(bf16[1024,6912,1,1]{0,1,3,2:T(8,128)(2,1)} %bitcast.121, bf16[8,2,1,1024]{3,0,2,1:T(8,128)(2,1)S(1)} %collective-permute-done.9, bf16[8,2,2,1024]{3,0,2,1:T(8,128)(2,1)S(1)} %copy.63, bf16[8,2,1,1024]{3,0,2,1:T(8,128)(2,1)S(1)} %collective-permute-done.8), kind=kOutput, calls=%fused_computation.125 | convolution fusion | flops 906100736 | bytes 16056320 | tf_op jit(solution)/shard_map/xyzd,dk->xyzk/dot_general | solution.py:83
  354.3 8.2 %fusion.132 = f32[32,1024]{1,0:T(8,128)} fusion(bf16[32,6912]{1,0:T(8,128)(2,1)S(1)} %dot_general.35, bf16[6912,1024]{1,0:T(8,128)(2,1)} %bitcast.119), kind=kOutput, calls=%fused_computation.273 | convolution fusion | flops 452984832 | bytes 14729216 | tf_op jit(solution)/shard_map/xyzk,kd->xyzd/dot_general | solution.py:111
  362.6 69.0 %all-reduce.17.cloned.1.call-done = f32[32,1024]{1,0:T(8,128)} async-done(((f32[32,1024]{1,0:T(8,128)}), f32[32,1024]{1,0:T(8,128)}) %all-reduce.17.cloned.1.call-update) | async-done | bytes 131088 | tf_op jit(solution)/shard_map/psum | solution.py:138
  431.6 3.6 convolution_convert_fusion
  435.3 11.0 %all_to_all.67 = bf16[8,4,2048]{2,1,0:T(4,128)(2,1)S(1)} all-to-all(bf16[8,4,2048]{2,1,0:T(4,128)(2,1)S(1)} %all_to_all.58), channel_id=1, replica_groups=mesh['groups'=2,'wide'=8,'narrow'=2] {'wide'}, dimensions={0} | all-to-all | bytes 262144 | tf_op jit(solution)/shard_map/all_to_all | solution.py:70
  453.6 4.3 collective-permute-done.13
  463.5 2.3 select_convert_fusion
  (161 shorter events, 50.0 us)
Async XLA Ops:
  6.5 114.2 %copy-start = (f32[1000,256]{1,0:T(8,128)S(1)}, f32[1000,256]{1,0:T(8,128)}, u32[]{:S(2)}) copy-start(f32[1000,256]{1,0:T(8,128)} %param.14) | copy-start | bytes 3072004
  6.5 110.6 %all-reduce.11.cloned.1.call-start = ((), (), s32[]{:S(2)}) async-start(), calls=%async_computation.4 | async-start | bytes 262144 | tf_op jit(solution)/shard_map/psum | solution.py:138
  7.5 6.8 %collective-permute-start = (bf16[32,1,16,16]{0,3,2,1:T(8,128)(2,1)S(1)}, bf16[32,1,16,16]{0,3,2,1:T(8,128)(2,1)S(1)}, u32[]{:S(2)}, u32[]{:S(2)}) collective-permute-start(bf16[32,1,16,16]{0,3,2,1:T(8,128)(2,1)S(1)} %get-tuple-element.14), channel_id=1, source_target_pairs={{0,2},{2,4},{4,6},{6,8},{8,10},{10,12},{12,14},{1,3},{3,5},{5,7},{... | collective-permute-start | bytes 49160 | tf_op jit(solution)/shard_map/ppermute | solution.py:17
  12.4 6.2 %collective-permute-start.1 = (bf16[32,1,16,16]{0,3,2,1:T(8,128)(2,1)S(1)}, bf16[32,1,16,16]{0,3,2,1:T(8,128)(2,1)S(1)}, u32[]{:S(2)}, u32[]{:S(2)}) collective-permute-start(bf16[32,1,16,16]{0,3,2,1:T(8,128)(2,1)S(1)} %get-tuple-element.13), channel_id=1, source_target_pairs={{2,0},{4,2},{6,4},{8,6},{10,8},{12,10},{14,12},{3,1},{5,3},{7,5},{... | collective-permute-start | bytes 49160 | tf_op jit(solution)/shard_map/ppermute | solution.py:19
  18.7 2.6 collective-permute-start.2
  20.0 3.2 collective-permute-start.3
  49.3 184.0 %all-reduce.13.cloned.1.call-start = ((), (), s32[]{:S(2)}) async-start(), calls=%async_computation.5 | async-start | bytes 262144 | tf_op jit(solution)/shard_map/psum | solution.py:138
  118.1 21.3 %collective-permute-start.4 = (bf16[8,2,1,1024]{3,0,2,1:T(8,128)(2,1)S(1)}, bf16[8,2,1,1024]{3,0,2,1:T(8,128)(2,1)S(1)}, u32[]{:S(2)}, u32[]{:S(2)}) collective-permute-start(bf16[8,2,1,1024]{3,0,2,1:T(8,128)(2,1)S(1)} %get-tuple-element.17), channel_id=1, source_target_pairs={{0,1},{2,3},{4,5},{6,7},{8,9},{10,11},{12,13},{14,15},{16,17},{18,... | collective-permute-start | bytes 98312 | tf_op jit(solution)/shard_map/ppermute | solution.py:17
  119.4 20.0 %collective-permute-start.5 = (bf16[8,2,1,1024]{3,0,2,1:T(8,128)(2,1)S(1)}, bf16[8,2,1,1024]{3,0,2,1:T(8,128)(2,1)S(1)}, u32[]{:S(2)}, u32[]{:S(2)}) collective-permute-start(bf16[8,2,1,1024]{3,0,2,1:T(8,128)(2,1)S(1)} %get-tuple-element.18), channel_id=1, source_target_pairs={{1,0},{3,2},{5,4},{7,6},{9,8},{11,10},{13,12},{15,14},{17,16},{19,... | collective-permute-start | bytes 98312 | tf_op jit(solution)/shard_map/ppermute | solution.py:19
  148.9 4.5 collective-permute-start.6
  151.9 3.1 collective-permute-start.7
  155.9 77.3 %copy-start.2 = (f32[32,1024]{1,0:T(8,128)S(1)}, f32[32,1024]{1,0:T(8,128)}, u32[]{:S(2)}) copy-start(f32[32,1024]{1,0:T(8,128)} %all-reduce.11.cloned.1.call-done) | copy-start | bytes 393220
  164.2 169.1 %all-reduce.15.cloned.1.call-start = ((), (), s32[]{:S(2)}) async-start(), calls=%async_computation.6 | async-start | bytes 262144 | tf_op jit(solution)/shard_map/psum | solution.py:138
  236.4 14.0 %copy-start.4 = (bf16[32,8,16,16]{0,3,2,1:T(8,128)(2,1)S(1)}, bf16[32,8,16,16]{0,3,2,1:T(8,128)(2,1)}, u32[]{:S(2)}) copy-start(bf16[32,8,16,16]{0,3,2,1:T(8,128)(2,1)} %param.10) | copy-start | bytes 393220
  265.8 165.8 %all-reduce.17.cloned.1.call-start = ((), (), s32[]{:S(2)}) async-start(), calls=%async_computation.7 | async-start | bytes 262144 | tf_op jit(solution)/shard_map/psum | solution.py:138
  334.3 2.6 collective-permute-start.8
  335.6 3.1 collective-permute-start.9
  348.2 3.6 collective-permute-start.10
  350.3 3.1 collective-permute-start.11
  354.3 77.3 %copy-start.3 = (f32[32,1024]{1,0:T(8,128)S(1)}, f32[32,1024]{1,0:T(8,128)}, u32[]{:S(2)}) copy-start(f32[32,1024]{1,0:T(8,128)} %all-reduce.15.cloned.1.call-done) | copy-start | bytes 393220
  449.5 4.0 collective-permute-start.12
  451.7 6.2 %collective-permute-start.13 = (bf16[32,1,16,16]{0,2,3,1:T(8,128)(2,1)S(1)}, bf16[32,1,16,16]{0,2,3,1:T(8,128)(2,1)S(1)}, u32[]{:S(2)}, u32[]{:S(2)}) collective-permute-start(bf16[32,1,16,16]{0,2,3,1:T(8,128)(2,1)S(1)} %get-tuple-element.12), channel_id=1, source_target_pairs={{2,0},{4,2},{6,4},{8,6},{10,8},{12,10},{14,12},{3,1},{5,3},{7,5},{... | collective-permute-start | bytes 49160 | tf_op jit(solution)/shard_map/ppermute | solution.py:19
  457.9 2.6 collective-permute-start.14
  459.2 3.1 collective-permute-start.15
  (3 other events, 5.3 us)
Sparse Core Ops, SparseCore 0:
  49.4 67.6 all-reduce.10
  164.3 68.8 all-reduce.12
  266.0 67.3 all-reduce.14
  362.7 68.8 all-reduce.16
where the time goes:
time: 475 us; the launch traced here: 473 us
  waiting for transfers between devices  290 us (61%)
  matrix products  54.5 us (11%)
  blocking collectives  44.8 us (9%)
  local copies, waits for them, and re-layouts  36.7 us (8%)
  starting transfers between devices  28.1 us (6%)
  between operations  14.8 us (3%)
  other arithmetic  4.77 us (1%)
    psum x4, waiting for transfers between devices, total_rows(): return lax.psum(partial_value, 'wide')  273 us
    all_to_all x2, blocking collectives, send_patches(): lax.all_to_all(to_patches(fine_field), 'wide', split_axis=1, concat_axis=...  22.6 us
    all_to_all x2, blocking collectives, return_patches(): lax.all_to_all(patch_rows, 'wide', split_axis=0, concat_axis=1, tiled=True)  22.2 us
    unnamed x65, local copies, waits for them, and re-layouts  20.7 us
    dot_general x2, matrix products, wide_input_conv(): jnp.einsum('xyzd,dk->xyzk', grown, weight_mat, preferred_element_type=jnp...  18.8 us
    ppermute x8, starting transfers between devices, extended(): lax.ppermute(tail, axis, [(i, (i + 1) % count) for i in range(ends)])  17.3 us
    dot_general x2, matrix products, narrow_input_conv(): jnp.einsum('xyzk,kd->xyzd', columns, weight_mat, preferred_element_type=j...  16.5 us
    ppermute x8, waiting for transfers between devices, extended(): lax.ppermute(head, axis, [((i + 1) % count, i) for i in range(ends)])  16 us
  transfers between devices with their start and end apart: 20, of which 13 were waited for; matrix products, arithmetic and copies ran while one was open for 4% of the time, Pallas kernels for 0%

commit v1 on v0

--- a/solution.py
+++ b/solution.py
@@ -4,6 +4,12 @@
 from jax.sharding import PartitionSpec as P
 
 PATCH = 8
+
+
+def gather_and_add(x, axis):
+    shards = lax.all_gather(x, axis, axis=0, tiled=False)
+    total = shards.sum(axis=0)
+    return total
 
 
 def extended(cells, sides, width):
@@ -135,7 +141,7 @@
     hidden_back = hidden_weight.transpose(0, 2, 1).reshape(27 * hidden_local, features)
 
     def total_rows(partial_value):
-        return lax.psum(partial_value, "wide")
+        return gather_and_add(partial_value, "wide")
 
     pre_act = fine_conv(volume, fine_weight, False)
     activated = jax.nn.silu(pre_act).astype(jnp.bfloat16)

time: 475 us -> 358 us (0.75)
  waiting for transfers between devices: 290 us -> 171 us
    psum x4 -> x0, waiting for transfers between devices: 273 us -> none  [total_rows(): return lax.psum(partial_value, 'wide')]
    all_gather x0 -> x4, waiting for transfers between devices: none -> 154 us  [gather_and_add(): shards = lax.all_gather(x, axis, axis=0, tiled=False)]
    reduce_sum x0 -> x4, other arithmetic: none -> 5.17 us  [gather_and_add(): total = shards.sum(axis=0)]
    unnamed x65 -> x61, local copies, waits for them, and re-layouts: 20.7 us -> 20.7 us
  transfers between devices with their start and end apart: 20 -> 20, of which waited for: 13 -> 13; matrix products, arithmetic and copies ran while one was open for 4% -> 6% of each run, Pallas kernels for 0% -> 0%
where the time goes in v1:
time: 358 us; the launch traced here: 357 us
  waiting for transfers between devices  171 us (48%)
  matrix products  54.3 us (15%)
  blocking collectives  43.7 us (12%)
  local copies, waits for them, and re-layouts  36.7 us (10%)
  starting transfers between devices  28.1 us (8%)
  between operations  14.8 us (4%)
  other arithmetic  8.13 us (2%)
    all_gather x4, waiting for transfers between devices, gather_and_add(): shards = lax.all_gather(x, axis, axis=0, tiled=False)  154 us
    all_to_all x2, blocking collectives, send_patches(): lax.all_to_all(to_patches(fine_field), 'wide', split_axis=1, concat_axis=...  22.6 us
    all_to_all x2, blocking collectives, return_patches(): lax.all_to_all(patch_rows, 'wide', split_axis=0, concat_axis=1, tiled=True)  21.1 us
    unnamed x61, local copies, waits for them, and re-layouts  20.7 us
    dot_general x2, matrix products, wide_input_conv(): jnp.einsum('xyzd,dk->xyzk', grown, weight_mat, preferred_element_type=jnp...  18.8 us
    ppermute x8, starting transfers between devices, extended(): lax.ppermute(tail, axis, [(i, (i + 1) % count) for i in range(ends)])  17.3 us
    dot_general x2, matrix products, narrow_input_conv(): jnp.einsum('xyzk,kd->xyzd', columns, weight_mat, preferred_element_type=j...  16.4 us
    ppermute x8, waiting for transfers between devices, extended(): lax.ppermute(head, axis, [((i + 1) % count, i) for i in range(ends)])  15.8 us
  transfers between devices with their start and end apart: 20, of which 13 were waited for; matrix products, arithmetic and copies ran while one was open for 6% of the time, Pallas kernels for 0%

profile of v1, /device:TPU:0, one launch (start us, length us, event | category | flops | bytes accessed | tf_op | source)
XLA Modules:
  0.0 356.7 jit_solution(193349132666889652)
XLA Ops:
  7.5 4.9 %collective-permute-start = (bf16[32,1,16,16]{0,3,2,1:T(8,128)(2,1)S(1)}, bf16[32,1,16,16]{0,3,2,1:T(8,128)(2,1)S(1)}, u32[]{:S(2)}, u32[]{:S(2)}) collective-permute-start(bf16[32,1,16,16]{0,3,2,1:T(8,128)(2,1)S(1)} %get-tuple-element.14), channel_id=1, source_target_pairs={{0,2},{2,4},{4,6},{6,8},{8,10},{10,12},{12,14},{1,3},{3,5},{5,7},{... | collective-permute-start | bytes 49160 | tf_op jit(solution)/shard_map/ppermute | solution.py:23
  15.4 3.2 collective-permute-done.1
  25.0 2.8 reshape.84
  28.8 2.4 fusion.20
  32.7 12.9 %all_to_all.64 = bf16[4,8,2048]{2,0,1:T(4,128)(2,1)S(1)} all-to-all(bf16[4,8,2048]{2,0,1:T(4,128)(2,1)S(1)} %copy.47), channel_id=1, replica_groups=mesh['groups'=2,'wide'=8,'narrow'=2] {'wide'}, dimensions={1} | all-to-all | bytes 262144 | tf_op jit(solution)/shard_map/all_to_all | solution.py:72
  45.6 3.7 %fusion.129 = f32[32,1024]{1,0:T(8,128)} fusion(bf16[32,2048]{1,0:T(8,128)(2,1)S(1)} %all_to_all.51, bf16[2048,1024]{1,0:T(8,128)(2,1)} %param.12), kind=kOutput, calls=%fused_computation.270 | convolution fusion | flops 134217728 | bytes 4456448 | tf_op jit(solution)/shard_map/dot_general | solution.py:149
  50.0 37.7 %all-gather.9.cloned.1.call-done = f32[256,1024]{1,0:T(8,128)} async-done(((f32[32,1024]{1,0:T(8,128)}), f32[256,1024]{1,0:T(8,128)}) %all-gather.9.cloned.1.call-update) | async-done | bytes 1048592 | tf_op jit(solution)/shard_map/all_gather | solution.py:10
  91.7 18.6 %copy.51 = bf16[27,1024,256]{1,2,0:T(8,128)(2,1)} copy(bf16[27,1024,256]{2,1,0:T(8,128)(2,1)} %param.13) | data formatting | bytes 28311552 | tf_op args[4]
  110.3 9.4 %fusion.50 = f32[8,2,4,6912]{3,0,2,1:T(8,128)S(1)} fusion(bf16[1024,6912,1,1]{0,1,3,2:T(8,128)(2,1)} %bitcast.122, bf16[8,2,1,1024]{3,0,2,1:T(8,128)(2,1)S(1)} %collective-permute-done.5, bf16[8,2,2,1024]{3,0,2,1:T(8,128)(2,1)S(1)} %copy.48, bf16[8,2,1,1024]{3,0,2,1:T(8,128)(2,1)S(1)} %collective-permute-done.4), kind=kOutput, calls=%fused_computation.119 | convolution fusion | flops 906100736 | bytes 16056320 | tf_op jit(solution)/shard_map/xyzd,dk->xyzk/dot_general | solution.py:89
  119.8 3.0 collective-permute-start.6
  126.9 8.2 %fusion.130 = f32[32,1024]{1,0:T(8,128)} fusion(bf16[32,6912]{1,0:T(8,128)(2,1)S(1)} %reshape.75, bf16[6912,1024]{1,0:T(8,128)(2,1)} %bitcast.124), kind=kOutput, calls=%fused_computation.271 | convolution fusion | flops 452984832 | bytes 14729216 | tf_op jit(solution)/shard_map/xyzk,kd->xyzd/dot_general | solution.py:117
  135.2 39.0 %all-gather.11.cloned.1.call-done = f32[256,1024]{1,0:T(8,128)} async-done(((f32[32,1024]{1,0:T(8,128)}), f32[256,1024]{1,0:T(8,128)}) %all-gather.11.cloned.1.call-update) | async-done | bytes 1048592 | tf_op jit(solution)/shard_map/all_gather | solution.py:10
  175.5 3.0 convolution_convert_fusion.1
  178.6 10.6 %all_to_all.65 = bf16[8,4,2048]{2,1,0:T(4,128)(2,1)S(1)} all-to-all(bf16[8,4,2048]{2,1,0:T(4,128)(2,1)S(1)} %all_to_all.52), channel_id=1, replica_groups=mesh['groups'=2,'wide'=8,'narrow'=2] {'wide'}, dimensions={0} | all-to-all | bytes 262144 | tf_op jit(solution)/shard_map/all_to_all | solution.py:76
  193.5 9.7 %all_to_all.66 = bf16[4,8,2048]{2,0,1:T(4,128)(2,1)S(1)} all-to-all(bf16[4,8,2048]{2,0,1:T(4,128)(2,1)S(1)} %copy.56), channel_id=1, replica_groups=mesh['groups'=2,'wide'=8,'narrow'=2] {'wide'}, dimensions={1} | all-to-all | bytes 262144 | tf_op jit(solution)/shard_map/all_to_all | solution.py:72
  203.2 4.2 %fusion.131 = f32[32,1024]{1,0:T(8,128)} fusion(bf16[32,2048]{1,0:T(8,128)(2,1)S(1)} %all_to_all.57, bf16[1024,2048]{1,0:T(8,128)(2,1)} %param.16), kind=kOutput, calls=%fused_computation.272 | convolution fusion | flops 134217728 | bytes 4456448 | tf_op jit(solution)/shard_map/nk,dk->nd/dot_general | solution.py:163
  207.5 38.0 %all-gather.13.cloned.1.call-done = f32[256,1024]{1,0:T(8,128)} async-done(((f32[32,1024]{1,0:T(8,128)}), f32[256,1024]{1,0:T(8,128)}) %all-gather.13.cloned.1.call-update) | async-done | bytes 1048592 | tf_op jit(solution)/shard_map/all_gather | solution.py:10
  251.3 9.4 %fusion.56 = f32[8,2,4,6912]{3,0,2,1:T(8,128)S(1)} fusion(bf16[1024,6912,1,1]{0,1,3,2:T(8,128)(2,1)} %bitcast.125, bf16[8,2,1,1024]{3,0,2,1:T(8,128)(2,1)S(1)} %collective-permute-done.9, bf16[8,2,2,1024]{3,0,2,1:T(8,128)(2,1)S(1)} %copy.57, bf16[8,2,1,1024]{3,0,2,1:T(8,128)(2,1)S(1)} %collective-permute-done.8), kind=kOutput, calls=%fused_computation.125 | convolution fusion | flops 906100736 | bytes 16056320 | tf_op jit(solution)/shard_map/xyzd,dk->xyzk/dot_general | solution.py:89
  266.9 8.2 %fusion.132 = f32[32,1024]{1,0:T(8,128)} fusion(bf16[32,6912]{1,0:T(8,128)(2,1)S(1)} %reshape.79, bf16[6912,1024]{1,0:T(8,128)(2,1)} %bitcast.123), kind=kOutput, calls=%fused_computation.273 | convolution fusion | flops 452984832 | bytes 14729216 | tf_op jit(solution)/shard_map/xyzk,kd->xyzd/dot_general | solution.py:117
  275.1 39.1 %all-gather.15.cloned.1.call-done = f32[256,1024]{1,0:T(8,128)} async-done(((f32[32,1024]{1,0:T(8,128)}), f32[256,1024]{1,0:T(8,128)}) %all-gather.15.cloned.1.call-update) | async-done | bytes 1048592 | tf_op jit(solution)/shard_map/all_gather | solution.py:10
  315.5 3.5 convolution_convert_fusion
  319.1 10.5 %all_to_all.67 = bf16[8,4,2048]{2,1,0:T(4,128)(2,1)S(1)} all-to-all(bf16[8,4,2048]{2,1,0:T(4,128)(2,1)S(1)} %all_to_all.58), channel_id=1, replica_groups=mesh['groups'=2,'wide'=8,'narrow'=2] {'wide'}, dimensions={0} | all-to-all | bytes 262144 | tf_op jit(solution)/shard_map/all_to_all | solution.py:76
  337.0 4.1 %collective-permute-done.13 = bf16[32,1,16,16]{0,2,3,1:T(8,128)(2,1)S(1)} collective-permute-done((bf16[32,1,16,16]{0,2,3,1:T(8,128)(2,1)S(1)}, bf16[32,1,16,16]{0,2,3,1:T(8,128)(2,1)S(1)}, u32[]{:S(2)}, u32[]{:S(2)}) %collective-permute-start.13) | collective-permute-done | bytes 16416 | tf_op jit(solution)/shard_map/ppermute | solution.py:25
  346.8 2.3 select_convert_fusion
  (161 shorter events, 53.6 us)
Async XLA Ops:
  6.5 85.1 %copy-start = (f32[1000,256]{1,0:T(8,128)S(1)}, f32[1000,256]{1,0:T(8,128)}, u32[]{:S(2)}) copy-start(f32[1000,256]{1,0:T(8,128)} %param.14) | copy-start | bytes 3072004
  6.5 81.1 %all-gather.9.cloned.1.call-start = ((), (), s32[]{:S(2)}) async-start(), calls=%async_computation.4 | async-start | bytes 1179648 | tf_op jit(solution)/shard_map/all_gather | solution.py:10
  7.5 6.8 %collective-permute-start = (bf16[32,1,16,16]{0,3,2,1:T(8,128)(2,1)S(1)}, bf16[32,1,16,16]{0,3,2,1:T(8,128)(2,1)S(1)}, u32[]{:S(2)}, u32[]{:S(2)}) collective-permute-start(bf16[32,1,16,16]{0,3,2,1:T(8,128)(2,1)S(1)} %get-tuple-element.14), channel_id=1, source_target_pairs={{0,2},{2,4},{4,6},{6,8},{8,10},{10,12},{12,14},{1,3},{3,5},{5,7},{... | collective-permute-start | bytes 49160 | tf_op jit(solution)/shard_map/ppermute | solution.py:23
  12.4 6.2 %collective-permute-start.1 = (bf16[32,1,16,16]{0,3,2,1:T(8,128)(2,1)S(1)}, bf16[32,1,16,16]{0,3,2,1:T(8,128)(2,1)S(1)}, u32[]{:S(2)}, u32[]{:S(2)}) collective-permute-start(bf16[32,1,16,16]{0,3,2,1:T(8,128)(2,1)S(1)} %get-tuple-element.13), channel_id=1, source_target_pairs={{2,0},{4,2},{6,4},{8,6},{10,8},{12,10},{14,12},{3,1},{5,3},{7,5},{... | collective-permute-start | bytes 49160 | tf_op jit(solution)/shard_map/ppermute | solution.py:25
  18.7 2.6 collective-permute-start.2
  20.0 3.2 collective-permute-start.3
  27.9 0.9 copy-start.3
  49.3 124.9 %all-gather.11.cloned.1.call-start = ((), (), s32[]{:S(2)}) async-start(), calls=%async_computation.5 | async-start | bytes 1179648 | tf_op jit(solution)/shard_map/all_gather | solution.py:10
  89.1 21.3 %collective-permute-start.4 = (bf16[8,2,1,1024]{3,0,2,1:T(8,128)(2,1)S(1)}, bf16[8,2,1,1024]{3,0,2,1:T(8,128)(2,1)S(1)}, u32[]{:S(2)}, u32[]{:S(2)}) collective-permute-start(bf16[8,2,1,1024]{3,0,2,1:T(8,128)(2,1)S(1)} %get-tuple-element.17), channel_id=1, source_target_pairs={{0,1},{2,3},{4,5},{6,7},{8,9},{10,11},{12,13},{14,15},{16,17},{18,... | collective-permute-start | bytes 98312 | tf_op jit(solution)/shard_map/ppermute | solution.py:23
  90.4 20.0 %collective-permute-start.5 = (bf16[8,2,1,1024]{3,0,2,1:T(8,128)(2,1)S(1)}, bf16[8,2,1,1024]{3,0,2,1:T(8,128)(2,1)S(1)}, u32[]{:S(2)}, u32[]{:S(2)}) collective-permute-start(bf16[8,2,1,1024]{3,0,2,1:T(8,128)(2,1)S(1)} %get-tuple-element.18), channel_id=1, source_target_pairs={{1,0},{3,2},{5,4},{7,6},{9,8},{11,10},{13,12},{15,14},{17,16},{19,... | collective-permute-start | bytes 98312 | tf_op jit(solution)/shard_map/ppermute | solution.py:25
  119.8 4.5 %collective-permute-start.6 = (bf16[8,2,1,256]{3,0,2,1:T(8,128)(2,1)S(1)}, bf16[8,2,1,256]{3,0,2,1:T(8,128)(2,1)S(1)}, u32[]{:S(2)}, u32[]{:S(2)}) collective-permute-start(bf16[8,2,1,256]{3,0,2,1:T(8,128)(2,1)S(1)} %get-tuple-element.21), channel_id=1, source_target_pairs={{0,1},{2,3},{4,5},{6,7},{8,9},{10,11},{12,13},{14,15},{16,17},{18,... | collective-permute-start | bytes 24584 | tf_op jit(solution)/shard_map/ppermute | solution.py:23
  122.9 3.1 collective-permute-start.7
  135.1 110.4 %all-gather.13.cloned.1.call-start = ((), (), s32[]{:S(2)}) async-start(), calls=%async_computation.6 | async-start | bytes 1179648 | tf_op jit(solution)/shard_map/all_gather | solution.py:10
  178.5 13.5 %copy-start.2 = (bf16[32,8,16,16]{0,3,2,1:T(8,128)(2,1)S(1)}, bf16[32,8,16,16]{0,3,2,1:T(8,128)(2,1)}, u32[]{:S(2)}) copy-start(bf16[32,8,16,16]{0,3,2,1:T(8,128)(2,1)} %param.10) | copy-start | bytes 393220
  207.5 106.7 %all-gather.15.cloned.1.call-start = ((), (), s32[]{:S(2)}) async-start(), calls=%async_computation.7 | async-start | bytes 1179648 | tf_op jit(solution)/shard_map/all_gather | solution.py:10
  246.9 2.6 collective-permute-start.8
  248.2 3.1 collective-permute-start.9
  260.8 3.6 %collective-permute-start.10 = (bf16[8,2,1,256]{3,0,2,1:T(8,128)(2,1)S(1)}, bf16[8,2,1,256]{3,0,2,1:T(8,128)(2,1)S(1)}, u32[]{:S(2)}, u32[]{:S(2)}) collective-permute-start(bf16[8,2,1,256]{3,0,2,1:T(8,128)(2,1)S(1)} %get-tuple-element.19), channel_id=1, source_target_pairs={{0,1},{2,3},{4,5},{6,7},{8,9},{10,11},{12,13},{14,15},{16,17},{18,... | collective-permute-start | bytes 24584 | tf_op jit(solution)/shard_map/ppermute | solution.py:23
  262.9 3.1 collective-permute-start.11
  332.8 4.2 %collective-permute-start.12 = (bf16[32,1,16,16]{0,2,3,1:T(8,128)(2,1)S(1)}, bf16[32,1,16,16]{0,2,3,1:T(8,128)(2,1)S(1)}, u32[]{:S(2)}, u32[]{:S(2)}) collective-permute-start(bf16[32,1,16,16]{0,2,3,1:T(8,128)(2,1)S(1)} %get-tuple-element.11), channel_id=1, source_target_pairs={{0,2},{2,4},{4,6},{6,8},{8,10},{10,12},{12,14},{1,3},{3,5},{5,7},{... | collective-permute-start | bytes 49160 | tf_op jit(solution)/shard_map/ppermute | solution.py:23
  335.0 6.2 %collective-permute-start.13 = (bf16[32,1,16,16]{0,2,3,1:T(8,128)(2,1)S(1)}, bf16[32,1,16,16]{0,2,3,1:T(8,128)(2,1)S(1)}, u32[]{:S(2)}, u32[]{:S(2)}) collective-permute-start(bf16[32,1,16,16]{0,2,3,1:T(8,128)(2,1)S(1)} %get-tuple-element.12), channel_id=1, source_target_pairs={{2,0},{4,2},{6,4},{8,6},{10,8},{12,10},{14,12},{3,1},{5,3},{7,5},{... | collective-permute-start | bytes 49160 | tf_op jit(solution)/shard_map/ppermute | solution.py:25
  341.1 2.6 collective-permute-start.14
  342.4 3.1 collective-permute-start.15
  346.8 3.4 copy-start.1
  (1 other events, 0.9 us)
Sparse Core Ops, SparseCore 0:
  49.4 38.2 all-gather.8
  135.3 38.8 all-gather.10
  207.6 37.8 all-gather.12
  275.3 38.8 all-gather.14
